TPU v7x, 32 devices: a whole 2x2x4 slice. The times are simulated.
32 devices in a mesh: chan: 8 (over z, core), grp: 4 (over y, x).
Axes of the slice: x: 2, y: 2, z: 4, core: 2. Of those that a mesh axis runs over, the one named last changes fastest.
Arguments:
- residual: bfloat16 [128, 4096], P('grp', 'chan'), may hold values from -6 to 6
- conv_input: bfloat16 [128, 8192], P('grp', 'chan'), may hold values from -6 to 6
- gate_input: bfloat16 [128, 8192], P('grp', 'chan'), may hold values from -6 to 6
- conv_state: bfloat16 [128, 3, 8192], P('grp', None, 'chan'), may hold values from -6 to 6
- conv_weight: float32 [4, 8192], P(None, 'chan'), may hold values from -3 to 3
- conv_bias: float32 [8192], P('chan'), may hold values from -1 to 1
- state_proj: bfloat16 [8192, 288], P('chan'), may hold values from -0.0625 to 0.0625
- step_proj: bfloat16 [256, 8192], P(None, 'chan'), may hold values from -0.375 to 0.375
- step_bias: float32 [8192], P('chan'), may hold values from -5 to -1
- decay_rate: float32 [16, 8192], P(None, 'chan'), may hold values from 1 to 16
- skip_gain: float32 [8192], P('chan'), may hold values from 0.5 to 1.5
- ssm_state: float32 [128, 16, 8192], P('grp', None, 'chan'), may hold values from -6 to 6
- out_proj: bfloat16 [8192, 4096], P('chan'), may hold values from -0.0625 to 0.0625
- router: bfloat16 [4096, 4], P('chan'), may hold values from -0.09375 to 0.09375
- expert_ids: int32 [128, 2], P('grp'), may hold values from 0 to 3, all different within a row; in each aligned block of 32 rows (0 to 31, 32 to 63, ...) at most 24 rows name the same one
- expert_gate: bfloat16 [4, 4096, 16384], P('grp', None, 'chan'), may hold values from -0.09375 to 0.09375
- expert_up: bfloat16 [4, 4096, 16384], P('grp', None, 'chan'), may hold values from -0.09375 to 0.09375
- expert_down: bfloat16 [4, 16384, 4096], P('grp', 'chan'), may hold values from -0.046875 to 0.046875
Outputs:
- layer_out: bfloat16 [128, 4096], P('grp', 'chan')
- new_state: float32 [128, 16, 8192], P('grp', None, 'chan')
Inputs may be any that keep to these rules, and one draw needn't show every extreme that they name: `expert_ids`: each request names two different experts; among the 32 requests of one group no expert is named more than 24 times, and in some group some expert is named exactly 24 times.
All inputs are finite; a program needn't handle non-finite values.
Results may differ from a plain program's by a relative error of at most 0.0056.
The roundings to bfloat16 on the way count: a program that leaves them out, or rounds other values in their place, can miss the bound.
Values may be sent and summed in bfloat16 or wider, within the bound.
A program may use at most 192 MiB of HBM per device.

v0:
```python
import jax
import jax.numpy as jnp
from jax import lax
from jax.sharding import PartitionSpec as P

EPSILON = 1e-06


def per_device(
    residual,
    conv_input,
    gate_input,
    conv_state,
    conv_weight,
    conv_bias,
    state_proj,
    step_proj,
    step_bias,
    decay_rate,
    skip_gain,
    ssm_state,
    out_proj,
    router,
    expert_ids,
    expert_gate,
    expert_up,
    expert_down,
):
    row_count = residual.shape[0]
    part_width = residual.shape[1]
    groups = lax.axis_size("grp")
    channels = lax.axis_size("chan")
    full_width = part_width * channels
    step_rank = step_proj.shape[0]
    nstates = decay_rate.shape[0]
    capacity = 3 * row_count // 4
    experts = router.shape[1]
    sharers = groups // experts
    window = conv_state.astype(jnp.float32)
    convolved = (
        conv_weight[0] * window[:, 0]
        + conv_weight[1] * window[:, 1]
        + conv_weight[2] * window[:, 2]
        + conv_weight[3] * conv_input.astype(jnp.float32)
        + conv_bias
    )
    inner_act = jax.nn.silu(convolved).astype(jnp.bfloat16)
    projected = lax.psum(jnp.dot(inner_act, state_proj, preferred_element_type=jnp.float32), "chan")
    step_raw = projected[:, :step_rank]
    input_mix = projected[:, step_rank : step_rank + nstates]
    output_mix = projected[:, step_rank + nstates :]
    step_norm = (
        step_raw * lax.rsqrt(jnp.mean(step_raw * step_raw, axis=1, keepdims=True) + EPSILON)
    ).astype(jnp.bfloat16)
    step_size = jax.nn.softplus(
        jnp.dot(step_norm, step_proj, preferred_element_type=jnp.float32) + step_bias
    )
    inner_wide = inner_act.astype(jnp.float32)
    decay_factor = jnp.exp(-step_size[:, None, :] * decay_rate[None, :, :])
    new_state = (
        decay_factor * ssm_state + (step_size * inner_wide)[:, None, :] * input_mix[:, :, None]
    )
    readout = jnp.sum(output_mix[:, :, None] * new_state, axis=1) + skip_gain * inner_wide
    gated_out = (readout * jax.nn.silu(gate_input.astype(jnp.float32))).astype(jnp.bfloat16)
    columns = out_proj
    mixer_part = lax.psum_scatter(
        lax.dot_general(
            columns, gated_out, (((0,), (1,)), ((), ())), preferred_element_type=jnp.float32
        ),
        "chan",
        scatter_dimension=0,
        tiled=True,
    )
    hidden_mid = residual.astype(jnp.float32) + mixer_part.T
    squares = jnp.sum(hidden_mid * hidden_mid, axis=1)
    router_wide = router.astype(jnp.float32)
    sum_squares = lax.psum(squares, "chan")
    inv_rms = lax.rsqrt(sum_squares / full_width + EPSILON)
    logits = lax.psum(
        jnp.dot(hidden_mid * inv_rms[:, None], router_wide, precision=lax.Precision.HIGHEST), "chan"
    )
    normed = (hidden_mid * inv_rms[:, None]).astype(jnp.bfloat16)
    labels = jnp.arange(experts, dtype=jnp.int32)
    chosen = jnp.sum(
        logits[:, None, :] * (expert_ids[:, :, None] == labels).astype(jnp.float32), axis=2
    )
    weight_first = jax.nn.sigmoid(chosen[:, 0] - chosen[:, 1])
    weight_second = 1.0 - weight_first
    flat_ids = expert_ids.reshape(-1)
    matches = (flat_ids[:, None] == labels).astype(jnp.int32)
    position = jnp.sum((jnp.cumsum(matches, axis=0) - matches) * matches, axis=1)
    target = flat_ids * capacity + position
    placing = (jnp.arange(experts * capacity, dtype=jnp.int32)[:, None] == target[None, :]).astype(
        jnp.bfloat16
    )
    repeated = jnp.repeat(normed, 2, axis=0)
    outgoing = jnp.dot(placing, repeated, preferred_element_type=jnp.float32).astype(jnp.bfloat16)
    copies = jnp.repeat(outgoing.reshape(experts, capacity, part_width), sharers, axis=0)
    incoming = lax.all_to_all(copies, "grp", split_axis=0, concat_axis=0, tiled=True)
    portion = lax.all_gather(
        incoming.reshape(groups * capacity, part_width), "chan", axis=1, tiled=True
    )
    gate_part = expert_gate[0]
    up_part = expert_up[0]
    gate_sum = jnp.dot(portion, gate_part, preferred_element_type=jnp.float32)
    up_sum = jnp.dot(portion, up_part, preferred_element_type=jnp.float32)
    hidden = (jax.nn.silu(gate_sum) * up_sum).astype(jnp.bfloat16)
    columns = expert_down[0]
    summed = lax.psum_scatter(
        lax.dot_general(
            columns, hidden, (((0,), (1,)), ((), ())), preferred_element_type=jnp.float32
        ),
        "chan",
        scatter_dimension=0,
        tiled=True,
    )
    answer = summed.T.astype(jnp.bfloat16)
    returned = lax.all_to_all(
        answer.reshape(groups, capacity, part_width), "grp", split_axis=0, concat_axis=0, tiled=True
    )
    combined = jnp.sum(
        returned.astype(jnp.float32).reshape(experts, sharers, capacity, part_width), axis=1
    )
    answers = lax.dot_general(
        placing.astype(jnp.float32),
        combined.reshape(experts * capacity, part_width),
        (((0,), (0,)), ((), ())),
        precision=lax.Precision.HIGHEST,
        preferred_element_type=jnp.float32,
    ).reshape(row_count, 2, part_width)
    layer_out = (
        hidden_mid + weight_first[:, None] * answers[:, 0] + weight_second[:, None] * answers[:, 1]
    ).astype(jnp.bfloat16)
    return (layer_out, new_state)


def solution(mesh):
    return jax.shard_map(
        per_device,
        mesh=mesh,
        in_specs=(
            P("grp", "chan"),
            P("grp", "chan"),
            P("grp", "chan"),
            P("grp", None, "chan"),
            P(None, "chan"),
            P("chan"),
            P("chan", None),
            P(None, "chan"),
            P("chan"),
            P(None, "chan"),
            P("chan"),
            P("grp", None, "chan"),
            P("chan", None),
            P("chan", None),
            P("grp", None),
            P("grp", None, "chan"),
            P("grp", None, "chan"),
            P("grp", "chan", None),
        ),
        out_specs=(P("grp", "chan"), P("grp", None, "chan")),
        check_vma=False,
    )
```

profile of v0, /device:TPU:0, one launch (start us, length us, event | category | flops | bytes accessed | tf_op | source)
XLA Modules:
  0.0 196.5 jit_solution(4262304531958366713)
XLA Ops:
  7.2 0.9 fusion.51
  8.1 1.0 convert_element_type.51
  9.1 0.9 multiply_convert_fusion
  10.0 0.3 fusion.52
  10.3 30.7 %psum.21 = f32[32,288]{1,0:T(8,128)S(1)} all-reduce(f32[32,288]{1,0:T(8,128)S(1)} %fusion.52), channel_id=1, replica_groups=mesh['chan'=8,'grp'=4] {'chan'}, use_global_device_ids=true, to_apply=%region_0.1 | all-reduce | flops 9216 | bytes 73728 | tf_op jit(solution)/shard_map/psum | solution.py:48
  41.2 1.3 fusion.49
  42.6 3.8 %multiply_reduce_fusion = (f32[32,1024]{1,0:T(8,128)S(1)}, f32[32,16,1024]{2,1,0:T(8,128)}) fusion(f32[32,16]{1,0:T(8,128)S(1)} %get-tuple-element.9, f32[32,16]{1,0:T(8,128)S(1)} %get-tuple-element.8, f32[32,1024]{1,0:T(8,128)S(1)} %get-tuple-element.7, f32[32,16,1024]{2,1,0:T(8,128)} %param.29, f32[16,1024]{1,0:T(8,128)} %param.27, ...), kind=kLoop, calls=%fused_computation.10 | loop fusion | flops 3112960 | bytes 4657152 | tf_op jit(solution)/shard_map/reduce_sum | solution.py:63
  46.3 5.8 %convolution_bitcast_fusion = f32[4096,32]{0,1:T(8,128)} fusion(bf16[1024,4096]{1,0:T(8,128)(2,1)} %param.30, f32[32,1024]{1,0:T(8,128)S(1)} %get-tuple-element.4, bf16[32,1024]{1,0:T(8,128)(2,1)S(1)} %multiply_convert_fusion, bf16[32,1024]{1,0:T(8,128)(2,1)} %param.20, f32[1024]{0:T(1024)} %param.28), kind=kOutput, calls=%fused_computation.7 | convolution fusion | flops 268763136 | bytes 9179136 | tf_op jit(solution)/shard_map/dot_general | solution.py:67
  52.6 0.2 select_reduce_fusion
  52.8 28.7 %reduce-scatter.3.cloned.1.call-done = f32[512,32]{0,1:T(8,128)} async-done(((f32[4096,32]{0,1:T(8,128)}), f32[512,32]{0,1:T(8,128)}) %reduce-scatter.3.cloned.1.call-update) | async-done | bytes 65552 | tf_op jit(solution)/shard_map/reduce_scatter | solution.py:66
  81.5 1.0 multiply_reduce_fusion.1
  82.4 13.7 %psum.22 = f32[32]{0:T(128)S(1)} all-reduce(f32[32]{0:T(128)S(1)} %multiply_reduce_fusion.1), channel_id=1, replica_groups=mesh['chan'=8,'grp'=4] {'chan'}, use_global_device_ids=true, to_apply=%region_5.6 | all-reduce | flops 32 | bytes 256 | tf_op jit(solution)/shard_map/psum | solution.py:77
  96.1 0.9 multiply_convert_fusion.1
  97.3 8.6 %all_to_all.10 = bf16[4,24,512]{2,1,0:T(8,128)(2,1)S(1)} all-to-all(bf16[4,24,512]{2,1,0:T(8,128)(2,1)S(1)} %bitcast.102), channel_id=1, replica_groups=mesh['chan'=8,'grp'=4] {'grp'}, dimensions={0} | all-to-all | bytes 196608 | tf_op jit(solution)/shard_map/all_to_all | solution.py:99
  105.9 15.8 %all_gather.3 = bf16[96,4096]{1,0:T(8,128)(2,1)S(1)} all-gather(bf16[96,512]{1,0:T(8,128)(2,1)S(1)} %bitcast.103), channel_id=1, replica_groups=mesh['chan'=8,'grp'=4] {'chan'}, dimensions={1}, use_global_device_ids=true | all-gather | bytes 884736 | tf_op jit(solution)/shard_map/all_gather | solution.py:100
  121.7 8.5 %fusion.4 = f32[96,2048]{1,0:T(8,128)S(1)} fusion(bf16[96,4096]{1,0:T(8,128)(2,1)S(1)} %all_gather.3, bf16[1,4096,2048]{2,1,0:T(8,128)(2,1)} %param.33), kind=kOutput, calls=%fused_computation.4 | convolution fusion | flops 1610612736 | bytes 18350080 | tf_op jit(solution)/shard_map/dot_general | solution.py:105
  130.3 17.2 %fusion.6 = f32[4096,96]{0,1:T(8,128)} fusion(bf16[1,2048,4096]{2,1,0:T(8,128)(2,1)} %param.35, bf16[96,4096]{1,0:T(8,128)(2,1)S(1)} %all_gather.3, bf16[1,4096,2048]{2,1,0:T(8,128)(2,1)} %param.34, f32[96,2048]{1,0:T(8,128)S(1)} %fusion.4), kind=kOutput, calls=%fused_computation.6 | convolution fusion | flops 3222405120 | bytes 36700160 | tf_op jit(solution)/shard_map/dot_general | solution.py:110
  147.7 0.2 fusion.39
  147.9 14.4 %psum.23 = f32[32,4]{0,1:T(4,128)S(1)} all-reduce(f32[32,4]{0,1:T(4,128)S(1)} %fusion.39), channel_id=1, replica_groups=mesh['chan'=8,'grp'=4] {'chan'}, use_global_device_ids=true, to_apply=%region_6.7 | all-reduce | flops 128 | bytes 1024 | tf_op jit(solution)/shard_map/psum | solution.py:79
  162.3 16.7 %reduce-scatter.5.cloned.1.call-done = f32[512,96]{0,1:T(8,128)} async-done(((f32[4096,96]{0,1:T(8,128)}), f32[512,96]{0,1:T(8,128)}) %reduce-scatter.5.cloned.1.call-update) | async-done | bytes 196624 | tf_op jit(solution)/shard_map/reduce_scatter | solution.py:109
  179.0 1.6 convert_element_type.62
  180.5 3.3 %all-to-all-start.1 = ((bf16[4,24,512]{2,1,0:T(8,128)(2,1)}), bf16[4,24,512]{2,1,0:T(8,128)(2,1)S(1)}, u32[]{:S(2)}, u32[]{:S(2)}) async-start(bf16[4,24,512]{2,1,0:T(8,128)(2,1)} %bitcast.17), calls=%async_computation.3 | async-start | bytes 196608 | tf_op jit(solution)/shard_map/all_to_all | solution.py:118
  183.8 4.9 %all-to-all-done.1 = bf16[4,24,512]{2,1,0:T(8,128)(2,1)S(1)} async-done(((bf16[4,24,512]{2,1,0:T(8,128)(2,1)}), bf16[4,24,512]{2,1,0:T(8,128)(2,1)S(1)}, u32[]{:S(2)}, u32[]{:S(2)}) %all-to-all-start.1) | async-done | bytes 98336 | tf_op jit(solution)/shard_map/all_to_all | solution.py:118
  188.9 0.7 fusion.34
  (33 shorter events, 1.2 us)
Async XLA Ops:
  7.2 2.8 %copy-start = (bf16[1024,288]{0,1:T(8,128)(2,1)S(1)}, bf16[1024,288]{0,1:T(8,128)(2,1)}, u32[]{:S(2)}) copy-start(bf16[1024,288]{0,1:T(8,128)(2,1)} %param.24) | copy-start | bytes 1769476
  7.2 74.3 %reduce-scatter.3.cloned.1.call-start = ((), (), s32[]{:S(2)}) async-start(), calls=%async_computation.4 | async-start | bytes 589824 | tf_op jit(solution)/shard_map/reduce_scatter | solution.py:66
  46.3 5.9 %copy-start.5 = (s32[32,2]{0,1:T(2,128)S(1)}, s32[32,2]{0,1:T(2,128)}, u32[]{:S(2)}) copy-start(s32[32,2]{0,1:T(2,128)} %param.32) | copy-start | bytes 772
  46.3 35.1 %copy-start.3 = (bf16[32,512]{1,0:T(8,128)(2,1)S(1)}, bf16[32,512]{1,0:T(8,128)(2,1)}, u32[]{:S(2)}) copy-start(bf16[32,512]{1,0:T(8,128)(2,1)} %param.18) | copy-start | bytes 98308
  52.1 126.8 %reduce-scatter.5.cloned.1.call-start = ((), (), s32[]{:S(2)}) async-start(), calls=%async_computation.5 | async-start | bytes 1769472 | tf_op jit(solution)/shard_map/reduce_scatter | solution.py:109
  130.2 17.4 %copy-start.2 = (f32[512,32]{0,1:T(8,128)S(1)}, f32[512,32]{0,1:T(8,128)}, u32[]{:S(2)}) copy-start(f32[512,32]{0,1:T(8,128)} %reduce-scatter.3.cloned.1.call-done) | copy-start | bytes 196612
  130.2 17.4 %copy-start.4 = (bf16[512,4]{0,1:T(4,128)(2,1)S(1)}, bf16[512,4]{0,1:T(4,128)(2,1)}, u32[]{:S(2)}) copy-start(bf16[512,4]{0,1:T(4,128)(2,1)} %param.31) | copy-start | bytes 12292
  130.2 59.4 %copy-start.1 = (bf16[1024,288]{0,1:T(8,128)(2,1)S(1)}, bf16[1024,288]{0,1:T(8,128)(2,1)}, u32[]{:S(2)}) copy-start(bf16[1024,288]{0,1:T(8,128)(2,1)} %param.24) | copy-start | bytes 1769476
  180.5 8.3 %all-to-all-start.1 = ((bf16[4,24,512]{2,1,0:T(8,128)(2,1)}), bf16[4,24,512]{2,1,0:T(8,128)(2,1)S(1)}, u32[]{:S(2)}, u32[]{:S(2)}) async-start(bf16[4,24,512]{2,1,0:T(8,128)(2,1)} %bitcast.17), calls=%async_computation.3 | async-start | bytes 196608 | tf_op jit(solution)/shard_map/all_to_all | solution.py:118
Sparse Core Ops, SparseCore 0:
  52.3 29.1 reduce-scatter.2
  147.6 31.2 reduce-scatter.4
where the time goes:
time: 197 us; the launch traced here: 196 us
  blocking collectives  83.2 us (42%)
  waiting for transfers between devices  50.3 us (26%)
  matrix products  33.7 us (17%)
  between operations  14.2 us (7%)
  other arithmetic  10.4 us (5%)
  starting transfers between devices  3.4 us (2%)
    psum x1, blocking collectives, per_device(): lax.psum(jnp.dot(inner_act, state_proj, preferred_element_type=jnp.float3...  30.7 us
    reduce_scatter x1, waiting for transfers between devices, per_device(): lax.psum_scatter(lax.dot_general(columns, gated_out, (((0,), (1,)), ((),...  28.7 us
    dot_general x1, matrix products, per_device(): lax.dot_general(columns, hidden, (((0,), (1,)), ((), ())), preferred_elem...  17.2 us
    reduce_scatter x1, waiting for transfers between devices, per_device(): lax.psum_scatter(lax.dot_general(columns, hidden, (((0,), (1,)), ((), ())...  16.7 us
    all_gather x1, blocking collectives, per_device(): lax.all_gather(incoming.reshape(groups * capacity, part_width), 'chan', a...  15.8 us
    psum x1, blocking collectives, per_device(): lax.psum(jnp.dot(hidden_mid * inv_rms[:, None], router_wide, precision=la...  14.4 us
    psum x1, blocking collectives, per_device(): sum_squares = lax.psum(squares, 'chan')  13.7 us
    all_to_all x1, blocking collectives, per_device(): lax.all_to_all(copies, 'grp', split_axis=0, concat_axis=0, tiled=True)  8.62 us
  transfers between devices with their start and end apart: 3, of which 3 were waited for; matrix products, arithmetic and copies ran while one was open for 0% of the time, Pallas kernels for 0%

commit v1 on v0

--- a/solution.py
+++ b/solution.py
@@ -4,6 +4,18 @@
 from jax.sharding import PartitionSpec as P
 
 EPSILON = 1e-06
+
+
+def gather_by_bits(x, axis, dim):
+    ways, here = (lax.axis_size(axis), lax.axis_index(axis))
+    grown, reach = (x, 1)
+    while reach < ways:
+        theirs = lax.ppermute(grown, axis, [(d, d ^ reach) for d in range(ways)])
+        mine_first = jnp.concatenate([grown, theirs], axis=dim)
+        theirs_first = jnp.concatenate([theirs, grown], axis=dim)
+        grown = jnp.where(here & reach == 0, mine_first, theirs_first)
+        reach = 2 * reach
+    return grown
 
 
 def per_device(
@@ -97,9 +109,7 @@
     outgoing = jnp.dot(placing, repeated, preferred_element_type=jnp.float32).astype(jnp.bfloat16)
     copies = jnp.repeat(outgoing.reshape(experts, capacity, part_width), sharers, axis=0)
     incoming = lax.all_to_all(copies, "grp", split_axis=0, concat_axis=0, tiled=True)
-    portion = lax.all_gather(
-        incoming.reshape(groups * capacity, part_width), "chan", axis=1, tiled=True
-    )
+    portion = gather_by_bits(incoming.reshape(groups * capacity, part_width), "chan", 1)
     gate_part = expert_gate[0]
     up_part = expert_up[0]
     gate_sum = jnp.dot(portion, gate_part, preferred_element_type=jnp.float32)

time: 197 us -> 207 us (1.051)
  waiting for transfers between devices: 50.3 us -> 78.4 us
  blocking collectives: 83.2 us -> 66.7 us
    ppermute x0 -> x3, waiting for transfers between devices: none -> 27.9 us  [gather_by_bits(): theirs = lax.ppermute(grown, axis, [(d, d ^ reach) for d in range(ways)])]
    all_gather x1 -> x0, blocking collectives: 15.8 us -> none  [per_device(): lax.all_gather(incoming.reshape(groups * capacity, part_width), 'chan', a...]
  transfers between devices with their start and end apart: 3 -> 6, of which waited for: 3 -> 6; matrix products, arithmetic and copies ran while one was open for 0% -> 0% of each run, Pallas kernels for 0% -> 0%
where the time goes in v1:
time: 207 us
  waiting for transfers between devices  78.4 us (38%)
  blocking collectives  66.7 us (32%)
  matrix products  33.3 us (16%)
  between operations  14.3 us (7%)
  other arithmetic  8.96 us (4%)
  starting transfers between devices  3.71 us (2%)
    psum x1, blocking collectives, per_device(): lax.psum(jnp.dot(inner_act, state_proj, preferred_element_type=jnp.float3...  30.7 us
    reduce_scatter x1, waiting for transfers between devices, per_device(): lax.psum_scatter(lax.dot_general(columns, gated_out, (((0,), (1,)), ((),...  28.7 us
    ppermute x3, waiting for transfers between devices, gather_by_bits(): theirs = lax.ppermute(grown, axis, [(d, d ^ reach) for d in range(ways)])  27.9 us
    dot_general x1, matrix products, per_device(): lax.dot_general(columns, hidden, (((0,), (1,)), ((), ())), preferred_elem...  17.3 us
    reduce_scatter x1, waiting for transfers between devices, per_device(): lax.psum_scatter(lax.dot_general(columns, hidden, (((0,), (1,)), ((), ())...  16.9 us
    psum x1, blocking collectives, per_device(): sum_squares = lax.psum(squares, 'chan')  13.7 us
    psum x1, blocking collectives, per_device(): lax.psum(jnp.dot(hidden_mid * inv_rms[:, None], router_wide, precision=la...  13.6 us
    all_to_all x1, blocking collectives, per_device(): lax.all_to_all(copies, 'grp', split_axis=0, concat_axis=0, tiled=True)  8.67 us
  transfers between devices with their start and end apart: 6, of which 6 were waited for; matrix products, arithmetic and copies ran while one was open for 0% of the time, Pallas kernels for 0%

profile of v1, /device:TPU:0, one launch (start us, length us, event | category | flops | bytes accessed | tf_op | source)
XLA Modules:
  0.0 206.7 jit_solution(4382513512648326720)
XLA Ops:
  7.3 0.9 fusion.50
  8.2 1.0 convert_element_type.51
  9.2 0.9 multiply_convert_fusion.2
  10.1 0.3 fusion.51
  10.4 30.7 %psum.21 = f32[32,288]{1,0:T(8,128)S(1)} all-reduce(f32[32,288]{1,0:T(8,128)S(1)} %fusion.51), channel_id=1, replica_groups=mesh['chan'=8,'grp'=4] {'chan'}, use_global_device_ids=true, to_apply=%region_0.1 | all-reduce | flops 9216 | bytes 73728 | tf_op jit(solution)/shard_map/psum | solution.py:60
  41.3 1.0 fusion.48
  42.3 2.2 %multiply_reduce_fusion = (f32[32,1024]{1,0:T(8,128)S(1)}, f32[32,16,1024]{2,1,0:T(8,128)}) fusion(f32[32,16]{1,0:T(8,128)S(1)} %get-tuple-element.9, f32[32,16]{1,0:T(8,128)S(1)} %get-tuple-element.8, f32[32,1024]{1,0:T(8,128)S(1)} %get-tuple-element.7, f32[32,16,1024]{2,1,0:T(8,128)S(1)} %copy-done.2, f32[16,1024]{1,0:T(8,128)S(1)} %copy-done.7, ...), kind=kLoop, calls=%fused_computation.8 | loop fusion | flops 3112960 | bytes 4657152 | tf_op jit(solution)/shard_map/reduce_sum | solution.py:75
  44.5 5.7 %convolution_bitcast_fusion = f32[4096,32]{0,1:T(8,128)} fusion(bf16[1024,4096]{1,0:T(8,128)(2,1)} %param.30, f32[32,1024]{1,0:T(8,128)S(1)} %get-tuple-element.4, bf16[32,1024]{1,0:T(8,128)(2,1)S(1)} %multiply_convert_fusion.2, bf16[32,1024]{1,0:T(8,128)(2,1)S(1)} %copy-done.6, f32[1024]{0:T(1024)S(1)} %copy-done.8), kind=kOutput, calls=%fused_computation.7 | convolution fusion | flops 268763136 | bytes 9179136 | tf_op jit(solution)/shard_map/dot_general | solution.py:79
  50.9 28.7 %reduce-scatter.3.cloned.1.call-done = f32[512,32]{0,1:T(8,128)} async-done(((f32[4096,32]{0,1:T(8,128)}), f32[512,32]{0,1:T(8,128)}) %reduce-scatter.3.cloned.1.call-update) | async-done | bytes 65552 | tf_op jit(solution)/shard_map/reduce_scatter | solution.py:78
  79.6 1.0 multiply_reduce_fusion.1
  80.5 13.7 %psum.22 = f32[32]{0:T(128)S(1)} all-reduce(f32[32]{0:T(128)S(1)} %multiply_reduce_fusion.1), channel_id=1, replica_groups=mesh['chan'=8,'grp'=4] {'chan'}, use_global_device_ids=true, to_apply=%region_5.6 | all-reduce | flops 32 | bytes 256 | tf_op jit(solution)/shard_map/psum | solution.py:89
  94.2 0.9 multiply_convert_fusion.3
  95.4 8.7 %all_to_all.10 = bf16[4,24,512]{2,1,0:T(8,128)(2,1)S(1)} all-to-all(bf16[4,24,512]{2,1,0:T(8,128)(2,1)S(1)} %bitcast.98), channel_id=1, replica_groups=mesh['chan'=8,'grp'=4] {'grp'}, dimensions={0} | all-to-all | bytes 196608 | tf_op jit(solution)/shard_map/all_to_all | solution.py:111
  104.1 1.3 collective-permute-done
  105.5 6.9 %collective-permute-done.1 = bf16[96,1024]{1,0:T(8,128)(2,1)S(1)} collective-permute-done((bf16[96,1024]{1,0:T(8,128)(2,1)S(1)}, bf16[96,1024]{1,0:T(8,128)(2,1)S(1)}, u32[]{:S(2)}, u32[]{:S(2)}) %collective-permute-start.1) | collective-permute-done | bytes 196640 | tf_op jit(solution)/shard_map/ppermute | solution.py:13
  112.6 19.7 %collective-permute-done.2 = bf16[96,2048]{1,0:T(8,128)(2,1)S(1)} collective-permute-done((bf16[96,2048]{1,0:T(8,128)(2,1)S(1)}, bf16[96,2048]{1,0:T(8,128)(2,1)S(1)}, u32[]{:S(2)}, u32[]{:S(2)}) %collective-permute-start.2) | collective-permute-done | bytes 393248 | tf_op jit(solution)/shard_map/ppermute | solution.py:13
  132.3 8.5 %fusion.2 = f32[96,2048]{1,0:T(8,128)S(1)} fusion(bf16[1,4096,2048]{2,1,0:T(8,128)(2,1)} %param.34, bf16[96,2048]{1,0:T(8,128)(2,1)S(1)} %collective-permute-done.2, bf16[96,2048]{1,0:T(8,128)(2,1)S(1)} %maximum_select_fusion.1, pred[]{:T(512)S(6)} %eq.73), kind=kOutput, calls=%fused_computation.2 | convolution fusion | flops 1614151680 | bytes 18350080 | tf_op jit(solution)/shard_map/dot_general | solution.py:116
  140.9 17.3 %fusion.6 = f32[4096,96]{0,1:T(8,128)} fusion(bf16[1,2048,4096]{2,1,0:T(8,128)(2,1)} %param.35, f32[96,2048]{1,0:T(8,128)S(1)} %fusion.2, bf16[1,4096,2048]{2,1,0:T(8,128)(2,1)} %param.33, bf16[96,2048]{1,0:T(8,128)(2,1)S(1)} %collective-permute-done.2, bf16[96,2048]{1,0:T(8,128)(2,1)S(1)} %maximum_select_fusion.1, pred[]{:T(512)S(6)} %eq.73), kind=kOutput, calls=%fused_computation.6 | convolution fusion | flops 3225944064 | bytes 36700160 | tf_op jit(solution)/shard_map/dot_general | solution.py:120
  158.5 13.6 %psum.23 = f32[32,4]{0,1:T(4,128)S(1)} all-reduce(f32[32,4]{0,1:T(4,128)S(1)} %fusion.35), channel_id=1, replica_groups=mesh['chan'=8,'grp'=4] {'chan'}, use_global_device_ids=true, to_apply=%region_6.7 | all-reduce | flops 128 | bytes 1024 | tf_op jit(solution)/shard_map/psum | solution.py:91
  172.2 16.9 %reduce-scatter.5.cloned.1.call-done = f32[512,96]{0,1:T(8,128)} async-done(((f32[4096,96]{0,1:T(8,128)}), f32[512,96]{0,1:T(8,128)}) %reduce-scatter.5.cloned.1.call-update) | async-done | bytes 196624 | tf_op jit(solution)/shard_map/reduce_scatter | solution.py:119
  189.0 1.6 convert_element_type.62
  190.6 3.5 %all-to-all-start.1 = ((bf16[4,24,512]{2,1,0:T(8,128)(2,1)}), bf16[4,24,512]{2,1,0:T(8,128)(2,1)S(1)}, u32[]{:S(2)}, u32[]{:S(2)}) async-start(bf16[4,24,512]{2,1,0:T(8,128)(2,1)} %bitcast.17), calls=%async_computation.3 | async-start | bytes 196608 | tf_op jit(solution)/shard_map/all_to_all | solution.py:128
  194.1 4.9 %all-to-all-done.1 = bf16[4,24,512]{2,1,0:T(8,128)(2,1)S(1)} async-done(((bf16[4,24,512]{2,1,0:T(8,128)(2,1)}), bf16[4,24,512]{2,1,0:T(8,128)(2,1)S(1)}, u32[]{:S(2)}, u32[]{:S(2)}) %all-to-all-start.1) | async-done | bytes 98336 | tf_op jit(solution)/shard_map/all_to_all | solution.py:128
  199.2 0.7 fusion.30
  (50 shorter events, 1.9 us)
Async XLA Ops:
  7.2 3.0 %copy-start = (bf16[1024,288]{0,1:T(8,128)(2,1)S(1)}, bf16[1024,288]{0,1:T(8,128)(2,1)}, u32[]{:S(2)}) copy-start(bf16[1024,288]{0,1:T(8,128)(2,1)} %param.24) | copy-start | bytes 1769476
  7.2 34.1 %copy-start.4 = (bf16[256,1024]{1,0:T(8,128)(2,1)S(1)}, bf16[256,1024]{1,0:T(8,128)(2,1)}, u32[]{:S(2)}) copy-start(bf16[256,1024]{1,0:T(8,128)(2,1)} %param.25) | copy-start | bytes 1572868
  7.2 35.1 %copy-start.7 = (f32[16,1024]{1,0:T(8,128)S(1)}, f32[16,1024]{1,0:T(8,128)}, u32[]{:S(2)}) copy-start(f32[16,1024]{1,0:T(8,128)} %param.27) | copy-start | bytes 196612
  7.2 35.1 %copy-start.2 = (f32[32,16,1024]{2,1,0:T(8,128)S(1)}, f32[32,16,1024]{2,1,0:T(8,128)}, u32[]{:S(2)}) copy-start(f32[32,16,1024]{2,1,0:T(8,128)} %param.29) | copy-start | bytes 6291460
  7.2 72.4 %reduce-scatter.3.cloned.1.call-start = ((), (), s32[]{:S(2)}) async-start(), calls=%async_computation.4 | async-start | bytes 589824 | tf_op jit(solution)/shard_map/reduce_scatter | solution.py:78
  42.3 2.2 %copy-start.6 = (bf16[32,1024]{1,0:T(8,128)(2,1)S(1)}, bf16[32,1024]{1,0:T(8,128)(2,1)}, u32[]{:S(2)}) copy-start(bf16[32,1024]{1,0:T(8,128)(2,1)} %param.20) | copy-start | bytes 196612
  42.3 2.2 %copy-start.8 = (f32[1024]{0:T(1024)S(1)}, f32[1024]{0:T(1024)}, u32[]{:S(2)}) copy-start(f32[1024]{0:T(1024)} %param.28) | copy-start | bytes 12292
  44.5 5.8 %copy-start.10 = (s32[32,2]{0,1:T(2,128)S(1)}, s32[32,2]{0,1:T(2,128)}, u32[]{:S(2)}) copy-start(s32[32,2]{0,1:T(2,128)} %param.32) | copy-start | bytes 772
  44.5 35.1 %copy-start.5 = (bf16[32,512]{1,0:T(8,128)(2,1)S(1)}, bf16[32,512]{1,0:T(8,128)(2,1)}, u32[]{:S(2)}) copy-start(bf16[32,512]{1,0:T(8,128)(2,1)} %param.18) | copy-start | bytes 98308
  50.3 138.8 %reduce-scatter.5.cloned.1.call-start = ((), (), s32[]{:S(2)}) async-start(), calls=%async_computation.5 | async-start | bytes 1769472 | tf_op jit(solution)/shard_map/reduce_scatter | solution.py:119
  104.1 1.3 collective-permute-start
  105.4 7.0 %collective-permute-start.1 = (bf16[96,1024]{1,0:T(8,128)(2,1)S(1)}, bf16[96,1024]{1,0:T(8,128)(2,1)S(1)}, u32[]{:S(2)}, u32[]{:S(2)}) collective-permute-start(bf16[96,1024]{1,0:T(8,128)(2,1)S(1)} %maximum_select_fusion.2), channel_id=1, source_target_pairs={{0,8},{4,12},{8,0},{12,4},{16,24},{20,28},{24,16},{28,20},{1,9},{5... | collective-permute-start | bytes 589832 | tf_op jit(solution)/shard_map/ppermute | solution.py:13
  112.6 19.7 %collective-permute-start.2 = (bf16[96,2048]{1,0:T(8,128)(2,1)S(1)}, bf16[96,2048]{1,0:T(8,128)(2,1)S(1)}, u32[]{:S(2)}, u32[]{:S(2)}) collective-permute-start(bf16[96,2048]{1,0:T(8,128)(2,1)S(1)} %maximum_select_fusion.1), channel_id=1, source_target_pairs={{0,16},{4,20},{8,24},{12,28},{16,0},{20,4},{24,8},{28,12},{1,17},{... | collective-permute-start | bytes 1179656 | tf_op jit(solution)/shard_map/ppermute | solution.py:13
  140.8 17.5 %copy-start.3 = (f32[512,32]{0,1:T(8,128)S(1)}, f32[512,32]{0,1:T(8,128)}, u32[]{:S(2)}) copy-start(f32[512,32]{0,1:T(8,128)} %reduce-scatter.3.cloned.1.call-done) | copy-start | bytes 196612
  140.8 17.5 %copy-start.9 = (bf16[512,4]{0,1:T(4,128)(2,1)S(1)}, bf16[512,4]{0,1:T(4,128)(2,1)}, u32[]{:S(2)}) copy-start(bf16[512,4]{0,1:T(4,128)(2,1)} %param.31) | copy-start | bytes 12292
  140.8 59.0 %copy-start.1 = (bf16[1024,288]{0,1:T(8,128)(2,1)S(1)}, bf16[1024,288]{0,1:T(8,128)(2,1)}, u32[]{:S(2)}) copy-start(bf16[1024,288]{0,1:T(8,128)(2,1)} %param.24) | copy-start | bytes 1769476
  190.6 8.4 %all-to-all-start.1 = ((bf16[4,24,512]{2,1,0:T(8,128)(2,1)}), bf16[4,24,512]{2,1,0:T(8,128)(2,1)S(1)}, u32[]{:S(2)}, u32[]{:S(2)}) async-start(bf16[4,24,512]{2,1,0:T(8,128)(2,1)} %bitcast.17), calls=%async_computation.3 | async-start | bytes 196608 | tf_op jit(solution)/shard_map/all_to_all | solution.py:128
Sparse Core Ops, SparseCore 0:
  50.4 29.1 reduce-scatter.2
  158.3 30.6 reduce-scatter.4
